TPU v7x, 256 devices: a whole 4x4x8 slice. The times are simulated.
256 devices in a mesh: ctx: 4 (over z_hi, core), exp: 64 (over x, y, z_lo).
Axes of the slice: x: 4, y: 4, z: 8 (z_hi: 2, z_lo: 4; z = z_hi * 4 + z_lo), core: 2. Of those that a mesh axis runs over, the one named last changes fastest.
Arguments:
- query: bfloat16 [64, 512, 1024], P('exp', 'ctx'), may hold values from -6 to 6
- key_states: bfloat16 [64, 512, 1024], P('exp', 'ctx'), may hold values from -6 to 6
- value_states: bfloat16 [64, 512, 1024], P('exp', 'ctx'), may hold values from -6 to 6
- segment_ids: int32 [64, 512], P('exp', 'ctx'), may hold values from 0 to 7, never falling along the last dimension, each value on 1 to 256 neighbouring positions
- out_weight: bfloat16 [1024, 2048], P('ctx'), may hold values from -0.1875 to 0.1875
- grad_out: bfloat16 [64, 512, 2048], P('exp', 'ctx'), may hold values from -6 to 6
- routes: int32 [64, 512, 4], P('exp', 'ctx'), may hold values from 0 to 63, all different within a row; in each aligned block of 128 rows (0 to 127, 128 to 255, ..., all dimensions but the last counted through in order) at most 10 rows name the same one
- route_gates: float32 [64, 512, 4], P('exp', 'ctx'), may hold values from 0.05 to 0.6
- w_gate: bfloat16 [64, 2048, 1408], P('exp', None, 'ctx'), may hold values from -0.125 to 0.125
- w_up: bfloat16 [64, 2048, 1408], P('exp', None, 'ctx'), may hold values from -0.125 to 0.125
- w_down: bfloat16 [64, 2048, 1408], P('exp', None, 'ctx'), may hold values from -0.15625 to 0.15625
- saved_gate: bfloat16 [64, 2560, 1408], P('exp', 'ctx'), may hold values from -8 to 8
- saved_up: bfloat16 [64, 2560, 1408], P('exp', 'ctx'), may hold values from -8 to 8
Outputs:
- d_hidden: bfloat16 [64, 512, 2048], P('exp', 'ctx')
- grad_query: bfloat16 [64, 512, 1024], P('exp', 'ctx')
- grad_key: bfloat16 [64, 512, 1024], P('exp', 'ctx')
- grad_value: bfloat16 [64, 512, 1024], P('exp', 'ctx')
Inputs may be any that keep to these rules, and one draw needn't show every extreme that they name: `routes`: each position names 4 different experts; within the 128 positions of one device no expert is named more than 10 times. `segment_ids`: never falling along a sequence; a segment covers 1 to 256 positions.
All inputs are finite; a program needn't handle non-finite values.
Results may differ from a plain program's by a relative error of at most 0.018.
Values may be sent and summed in bfloat16 or wider, within the bound.
No kernel may reach another device: no remote copies, remote signals or barrier semaphores. Data moves between devices by JAX's collectives and lax.ppermute only.
A program may use at most 128 MiB of HBM per device.

v0:
```python
import math

import jax
import jax.numpy as jnp
from jax import lax
from jax.sharding import PartitionSpec as P

D = 2048
HEADS = 8
HD = 128


def slot_numbers(expert_ids, experts_all):
    table = (expert_ids[..., None] == jnp.arange(experts_all, dtype=jnp.int32)).astype(jnp.int32)
    earlier = jnp.cumsum(table, axis=-2) - table
    return jnp.sum(earlier * table, axis=-1)


def expert_grads(grad_out, routes, route_gates, w_gate, w_up, w_down, saved_gate, saved_up):
    exp_count = lax.axis_size("exp")
    experts_here = w_gate.shape[0]
    rows_in = saved_gate.shape[1]
    capacity = rows_in // exp_count
    expert_ids = routes[0]
    slot_index = slot_numbers(expert_ids.reshape(-1), experts_here * exp_count).reshape(
        expert_ids.shape
    )
    owners = expert_ids // experts_here
    local_index = expert_ids % experts_here
    scaled = (route_gates[0][:, :, None] * grad_out[0][:, None, :].astype(jnp.float32)).astype(
        jnp.bfloat16
    )
    outgoing = jnp.zeros((experts_here, exp_count, capacity, D), jnp.bfloat16)
    outgoing = outgoing.at[local_index, owners, slot_index].set(scaled)
    arrived = lax.all_to_all(outgoing, "exp", split_axis=1, concat_axis=1, tiled=True)
    routed_rows = arrived.reshape(experts_here, rows_in, D)
    gate_piece = lax.all_gather(w_gate, "ctx", axis=2, tiled=True)
    up_piece = lax.all_gather(w_up, "ctx", axis=2, tiled=True)
    down_piece = lax.all_gather(w_down, "ctx", axis=2, tiled=True)
    gate_pre = saved_gate.astype(jnp.float32)
    up_pre = saved_up.astype(jnp.float32)
    hidden_grad = jnp.einsum(
        "erd,edf->erf", routed_rows, down_piece, preferred_element_type=jnp.float32
    )
    sigmoid_gate = jax.nn.sigmoid(gate_pre)
    grad_gate = (
        hidden_grad * up_pre * sigmoid_gate * (1.0 + gate_pre * (1.0 - sigmoid_gate))
    ).astype(jnp.bfloat16)
    grad_up = (hidden_grad * gate_pre * sigmoid_gate).astype(jnp.bfloat16)
    running = jnp.einsum("erf,edf->erd", grad_gate, gate_piece, preferred_element_type=jnp.float32)
    summed = running + jnp.einsum(
        "erf,edf->erd", grad_up, up_piece, preferred_element_type=jnp.float32
    )
    leaving = summed.astype(jnp.bfloat16).reshape(experts_here, exp_count, capacity, D)
    returned = lax.all_to_all(leaving, "exp", split_axis=1, concat_axis=1, tiled=True)
    picked = returned[local_index, owners, slot_index].astype(jnp.float32)
    d_hidden = (grad_out[0].astype(jnp.float32) + jnp.sum(picked, axis=1)).astype(jnp.bfloat16)
    return d_hidden[None]


def attention_weights(query, key_states, value_states, segment_ids):
    tokens_here = query.shape[1]
    scale = 1.0 / math.sqrt(HD)
    segment_marks = segment_ids.astype(jnp.bfloat16)
    key_all, value_all, segment_all = (
        lax.all_gather(key_states, "ctx", axis=1, tiled=True),
        lax.all_gather(value_states, "ctx", axis=1, tiled=True),
        lax.all_gather(segment_marks, "ctx", axis=1, tiled=True),
    )
    length_all = key_all.shape[1]
    queries = query[0].reshape(tokens_here, HEADS, HD)
    keys_all = key_all[0].reshape(length_all, HEADS, HD)
    values_all = value_all[0].reshape(length_all, HEADS, HD)
    scores = (
        jnp.einsum("ihd,jhd->hij", queries, keys_all, preferred_element_type=jnp.float32) * scale
    )
    query_pos = lax.axis_index("ctx") * tokens_here + jnp.arange(tokens_here, dtype=jnp.int32)
    key_pos = jnp.arange(length_all, dtype=jnp.int32)
    segment_here = segment_ids[0].astype(jnp.float32)
    segment_keys = segment_all[0].astype(jnp.float32)
    causal = key_pos[None, :] <= query_pos[:, None]
    image = (segment_here[:, None] == segment_keys[None, :]) & (jnp.mod(segment_here, 2.0) == 1.0)[
        :, None
    ]
    allowed = (causal | image)[None]
    scores = jnp.where(allowed, scores, -jnp.inf)
    row_max = jnp.max(scores, axis=2, keepdims=True)
    expd = jnp.exp(scores - row_max)
    row_total = jnp.sum(expd, axis=2, keepdims=True)
    probs = expd / row_total
    probs_b = probs.astype(jnp.bfloat16)
    attn_out = jnp.einsum("hij,jhd->ihd", probs_b, values_all, preferred_element_type=jnp.float32)
    return (
        probs,
        probs_b,
        attn_out,
        queries,
        keys_all,
        values_all,
        row_max,
        row_total,
        segment_keys,
    )


def output_grad(d_hidden, out_weight):
    return lax.dot_general(
        d_hidden[0],
        lax.all_gather(out_weight, "ctx", axis=0, tiled=True),
        (((1,), (1,)), ((), ())),
        preferred_element_type=jnp.float32,
    ).astype(jnp.bfloat16)


def attention_grads(grad_attn, attention_parts):
    probs, probs_b, attn_out, queries, keys_all, values_all, row_max, row_total, segment_keys = (
        attention_parts
    )
    tokens_here = grad_attn.shape[0]
    features = HEADS * HD
    scale = 1.0 / math.sqrt(HD)
    grads = grad_attn.reshape(tokens_here, HEADS, HD)
    delta = jnp.sum(grads.astype(jnp.float32) * attn_out, axis=2)
    dprobs = jnp.einsum("ihd,jhd->hij", grads, values_all, preferred_element_type=jnp.float32)
    dscores = (probs * (dprobs - delta.T[:, :, None])).astype(jnp.bfloat16)
    grad_query = (
        jnp.einsum("hij,jhd->ihd", dscores, keys_all, preferred_element_type=jnp.float32) * scale
    )
    grad_query = grad_query.astype(jnp.bfloat16).reshape(1, tokens_here, features)
    key_part = (
        jnp.einsum("hij,ihd->jhd", dscores, queries, preferred_element_type=jnp.float32) * scale
    )
    value_part = jnp.einsum("hij,ihd->jhd", probs_b, grads, preferred_element_type=jnp.float32)
    summed = lax.psum_scatter(
        jnp.concatenate(
            [
                key_part.reshape(lax.axis_size("ctx") * tokens_here, features),
                value_part.reshape(lax.axis_size("ctx") * tokens_here, features),
            ],
            axis=1,
        ).astype(jnp.bfloat16),
        "ctx",
        scatter_dimension=0,
        tiled=True,
    ).astype(jnp.float32)
    grad_key = summed[:, :features].astype(jnp.bfloat16)[None]
    grad_value = summed[:, features:].astype(jnp.bfloat16)[None]
    return (grad_query, grad_key, grad_value)


def on_device(
    query,
    key_states,
    value_states,
    segment_ids,
    out_weight,
    grad_out,
    routes,
    route_gates,
    w_gate,
    w_up,
    w_down,
    saved_gate,
    saved_up,
):
    d_hidden = expert_grads(
        grad_out, routes, route_gates, w_gate, w_up, w_down, saved_gate, saved_up
    )
    attention_parts = attention_weights(query, key_states, value_states, segment_ids)
    grad_attn = output_grad(d_hidden, out_weight)
    grad_query, grad_key, grad_value = attention_grads(grad_attn, attention_parts)
    return (d_hidden, grad_query, grad_key, grad_value)


def solution(mesh):
    in_specs = (
        P("exp", "ctx", None),
        P("exp", "ctx", None),
        P("exp", "ctx", None),
        P("exp", "ctx"),
        P("ctx", None),
        P("exp", "ctx", None),
        P("exp", "ctx", None),
        P("exp", "ctx", None),
        P("exp", None, "ctx"),
        P("exp", None, "ctx"),
        P("exp", None, "ctx"),
        P("exp", "ctx", None),
        P("exp", "ctx", None),
    )
    out_specs = (
        P("exp", "ctx", None),
        P("exp", "ctx", None),
        P("exp", "ctx", None),
        P("exp", "ctx", None),
    )
    return jax.shard_map(
        on_device, mesh=mesh, in_specs=in_specs, out_specs=out_specs, check_vma=False
    )
```

profile of v0, /device:TPU:1, one launch (start us, length us, event | category | flops | bytes accessed | tf_op | source)
XLA Modules:
  0.0 602.1 jit_solution(12782079596518744287)
XLA Ops:
  15.1 67.3 %scatter_fusion = bf16[64,10,2048]{2,0,1:T(8,128)(2,1)S(1)} fusion(bf16[64,10,2048]{2,0,1:T(8,128)(2,1)S(1)} %broadcast.195, s32[512]{0:T(512)S(1)} %reshape.248, bf16[512,2048]{1,0:T(8,128)(2,1)} %reshape.250), kind=kCustom, calls=%fused_computation.1 | custom fusion | bytes 6295552 | tf_op jit(solution)/shard_map/scatter | solution.py:34
  82.4 3.6 copy.53
  86.0 12.9 %all-to-all-start = ((bf16[1,64,10,2048]{3,2,0,1:T(8,128)(2,1)}), bf16[1,64,10,2048]{3,2,0,1:T(8,128)(2,1)}, u32[]{:S(2)}, u32[]{:S(2)}) async-start(bf16[1,64,10,2048]{3,2,0,1:T(8,128)(2,1)} %copy.53), calls=%async_computation | async-start | bytes 8388608 | tf_op jit(solution)/shard_map/all_to_all | solution.py:35
  100.5 216.8 %all-to-all-done = bf16[1,64,10,2048]{3,2,0,1:T(8,128)(2,1)} async-done(((bf16[1,64,10,2048]{3,2,0,1:T(8,128)(2,1)}), bf16[1,64,10,2048]{3,2,0,1:T(8,128)(2,1)}, u32[]{:S(2)}, u32[]{:S(2)}) %all-to-all-start) | async-done | bytes 2621472 | tf_op jit(solution)/shard_map/all_to_all | solution.py:35
  317.3 4.1 reshape.227
  321.4 8.7 %fusion.5 = f32[640,1408]{1,0:T(8,128)} fusion(bf16[640,2048]{1,0:T(8,128)(2,1)S(1)} %reshape.227, bf16[1,2048,1408]{1,2,0:T(8,128)(2,1)} %all-gather.7.cloned.1.call-done), kind=kOutput, calls=%fused_computation.7 | convolution fusion | flops 3690987520 | bytes 11993088 | tf_op jit(solution)/shard_map/erd,edf->erf/dot_general | solution.py:42
  330.1 10.9 %fusion.1 = f32[640,2048]{1,0:T(8,128)} fusion(bf16[1,2048,1408]{1,2,0:T(8,128)(2,1)} %all-gather.11.cloned.1.call-done, bf16[1,640,1408]{2,1,0:T(8,128)(2,1)} %param.24, f32[640,1408]{1,0:T(8,128)} %fusion.5), kind=kOutput, calls=%fused_computation.3 | convolution fusion | flops 3697295360 | bytes 16416768 | tf_op jit(solution)/shard_map/erf,edf->erd/dot_general | solution.py:51
  341.1 12.2 %add_convert_fusion = bf16[640,2048]{1,0:T(8,128)(2,1)S(1)} fusion(f32[640,2048]{1,0:T(8,128)} %fusion.1, bf16[1,2048,1408]{1,2,0:T(8,128)(2,1)} %all-gather.9.cloned.1.call-done, bf16[1,640,1408]{2,1,0:T(8,128)(2,1)} %param.24, f32[640,1408]{1,0:T(8,128)} %fusion.5, bf16[1,640,1408]{2,1,0:T(8,128)(2,1)} %param.25), kind=kOutput, calls=%fused_computation.12 | convolution fusion | flops 3704422400 | bytes 20840448 | tf_op jit(solution)/shard_map/erf,edf->erd/dot_general | solution.py:50
  353.3 2.8 reshape.233
  356.1 14.4 %all-to-all-start.1 = ((bf16[1,64,10,2048]{3,2,0,1:T(8,128)(2,1)}), bf16[1,64,10,2048]{3,2,0,1:T(8,128)(2,1)}, u32[]{:S(2)}, u32[]{:S(2)}) async-start(bf16[1,64,10,2048]{3,2,0,1:T(8,128)(2,1)} %bitcast.115), calls=%async_computation.1 | async-start | bytes 8388608 | tf_op jit(solution)/shard_map/all_to_all | solution.py:55
  371.6 102.8 %all_gather.24 = bf16[1,512]{1,0:T(2,128)(2,1)S(1)} all-gather(bf16[1,128]{1,0:T(2,128)(2,1)S(1)} %get-tuple-element.21), channel_id=1, replica_groups=mesh['ctx'=4,'exp'=64] {'ctx'}, dimensions={1}, use_global_device_ids=true | all-gather | bytes 1280 | tf_op jit(solution)/shard_map/all_gather | solution.py:68
  474.8 3.5 fusion.48
  478.3 18.6 %all-to-all-done.1 = bf16[1,64,10,2048]{3,2,0,1:T(8,128)(2,1)} async-done(((bf16[1,64,10,2048]{3,2,0,1:T(8,128)(2,1)}), bf16[1,64,10,2048]{3,2,0,1:T(8,128)(2,1)}, u32[]{:S(2)}, u32[]{:S(2)}) %all-to-all-start.1) | async-done | bytes 2621472 | tf_op jit(solution)/shard_map/all_to_all | solution.py:55
  496.9 3.6 copy.55
  500.6 10.1 %gather_fusion = bf16[512,2048]{1,0:T(8,128)(2,1)} fusion(bf16[1,64,10,2048]{3,1,2,0:T(8,128)(2,1)S(1)} %copy.55, s32[512]{0:T(512)S(1)} %reshape.240), kind=kCustom, calls=%fused_computation | custom fusion | bytes 4200448 | tf_op jit(solution)/shard_map/gather | solution.py:56
  510.7 4.7 reshape.254
  515.4 4.8 reduce_sum.39
  520.3 3.7 convolution_convert_fusion.1
  524.2 3.1 convolution_convert_fusion
  527.3 2.5 fusion.25
  532.1 2.3 copy.65
  534.4 2.3 copy.66
  536.7 3.1 pad_maximum_fusion
  543.2 50.1 %reduce-scatter.2.cloned.1.call-done = bf16[128,2048]{1,0:T(8,128)(2,1)} async-done(((bf16[512,2048]{1,0:T(8,128)(2,1)}), bf16[128,2048]{1,0:T(8,128)(2,1)}) %reduce-scatter.2.cloned.1.call-update) | async-done | bytes 524304 | tf_op jit(solution)/shard_map/reduce_scatter | solution.py:134
  (71 shorter events, 18.5 us)
Async XLA Ops:
  7.2 2.3 copy-start.4
  7.2 4.5 copy-start.5
  7.2 4.6 copy-start
  7.2 314.2 %all-gather.7.cloned.1.call-start = ((), (), s32[]{:S(2)}) async-start(), calls=%async_computation.3 | async-start | bytes 7208960 | tf_op jit(solution)/shard_map/all_gather | solution.py:39
  7.9 322.2 %all-gather.11.cloned.1.call-start = ((), (), s32[]{:S(2)}) async-start(), calls=%async_computation.5 | async-start | bytes 7208960 | tf_op jit(solution)/shard_map/all_gather | solution.py:38
  8.7 332.4 %all-gather.9.cloned.1.call-start = ((), (), s32[]{:S(2)}) async-start(), calls=%async_computation.4 | async-start | bytes 7208960 | tf_op jit(solution)/shard_map/all_gather | solution.py:37
  86.0 13.0 %copy-start.1 = (bf16[1,128,1024]{2,1,0:T(8,128)(2,1)S(1)}, bf16[1,128,1024]{2,1,0:T(8,128)(2,1)}, u32[]{:S(2)}) copy-start(bf16[1,128,1024]{2,1,0:T(8,128)(2,1)} %param.14) | copy-start | bytes 786436
  86.0 231.3 %all-to-all-start = ((bf16[1,64,10,2048]{3,2,0,1:T(8,128)(2,1)}), bf16[1,64,10,2048]{3,2,0,1:T(8,128)(2,1)}, u32[]{:S(2)}, u32[]{:S(2)}) async-start(bf16[1,64,10,2048]{3,2,0,1:T(8,128)(2,1)} %copy.53), calls=%async_computation | async-start | bytes 8388608 | tf_op jit(solution)/shard_map/all_to_all | solution.py:35
  99.0 375.8 %all-gather.13.cloned.1.call-start = ((), (), s32[]{:S(2)}) async-start(), calls=%async_computation.6 | async-start | bytes 1310720 | tf_op jit(solution)/shard_map/all_gather | solution.py:66
  99.9 420.4 %all-gather.15.cloned.1.call-start = ((), (), s32[]{:S(2)}) async-start(), calls=%async_computation.7 | async-start | bytes 5242880 | tf_op jit(solution)/shard_map/all_gather | solution.py:109
  356.1 14.5 %copy-start.2 = (bf16[1,128,1024]{2,1,0:T(8,128)(2,1)S(1)}, bf16[1,128,1024]{2,1,0:T(8,128)(2,1)}, u32[]{:S(2)}) copy-start(bf16[1,128,1024]{2,1,0:T(8,128)(2,1)} %param.15) | copy-start | bytes 786436
  356.1 15.5 %copy-start.7 = (s32[1,128]{1,0:T(1,128)S(1)}, s32[1,128]{1,0:T(1,128)}, u32[]{:S(2)}) copy-start(s32[1,128]{1,0:T(1,128)} %param.16) | copy-start | bytes 1540
  356.1 118.4 %copy-start.3 = (bf16[1,128,1024]{2,1,0:T(8,128)(2,1)S(1)}, bf16[1,128,1024]{2,1,0:T(8,128)(2,1)}, u32[]{:S(2)}) copy-start(bf16[1,128,1024]{2,1,0:T(8,128)(2,1)} %param.13) | copy-start | bytes 786436
  356.1 140.9 %all-to-all-start.1 = ((bf16[1,64,10,2048]{3,2,0,1:T(8,128)(2,1)}), bf16[1,64,10,2048]{3,2,0,1:T(8,128)(2,1)}, u32[]{:S(2)}, u32[]{:S(2)}) async-start(bf16[1,64,10,2048]{3,2,0,1:T(8,128)(2,1)} %bitcast.115), calls=%async_computation.1 | async-start | bytes 8388608 | tf_op jit(solution)/shard_map/all_to_all | solution.py:55
  370.5 156.8 %all-gather.17.cloned.1.call-start = ((), (), s32[]{:S(2)}) async-start(), calls=%async_computation.8 | async-start | bytes 1310720 | tf_op jit(solution)/shard_map/all_gather | solution.py:67
  371.4 222.0 %reduce-scatter.2.cloned.1.call-start = ((), (), s32[]{:S(2)}) async-start(), calls=%async_computation.9 | async-start | bytes 2621440 | tf_op jit(solution)/shard_map/reduce_scatter | solution.py:134
  527.3 2.6 copy-start.6
  527.3 2.9 copy-start.8
Sparse Core Ops, SparseCore 0:
  9.8 88.3 all-gather.6
  100.0 94.8 all-gather.10
  196.7 78.4 all-gather.8
  277.5 54.4 all-gather.12
  333.6 57.8 all-gather.14
  393.8 63.0 all-gather.16
  539.9 53.4 reduce-scatter.1
where the time goes:
time: 604 us; the launch traced here: 602 us
  waiting for transfers between devices  288 us (48%)
  local copies, waits for them, and re-layouts  109 us (18%)
  blocking collectives  103 us (17%)
  matrix products  48.3 us (8%)
  starting transfers between devices  27.8 us (5%)
  between operations  14.4 us (2%)
  other arithmetic  11.4 us (2%)
    all_to_all x1, waiting for transfers between devices, expert_grads(): lax.all_to_all(outgoing, 'exp', split_axis=1, concat_axis=1, tiled=True)  217 us
    all_gather x1, blocking collectives, attention_weights(): lax.all_gather(segment_marks, 'ctx', axis=1, tiled=True)  103 us
    scatter x2, local copies, waits for them, and re-layouts, expert_grads(): outgoing = outgoing.at[local_index, owners, slot_index].set(scaled)  70.9 us
    reduce_scatter x1, waiting for transfers between devices, attention_grads(): lax.psum_scatter(jnp.concatenate([key_part.reshape(lax.axis_size('ctx') *...  50.1 us
    all_to_all x1, waiting for transfers between devices, expert_grads(): lax.all_to_all(leaving, 'exp', split_axis=1, concat_axis=1, tiled=True)  18.6 us
    all_to_all x1, starting transfers between devices, expert_grads(): lax.all_to_all(leaving, 'exp', split_axis=1, concat_axis=1, tiled=True)  14.4 us
    all_to_all x1, starting transfers between devices, expert_grads(): lax.all_to_all(outgoing, 'exp', split_axis=1, concat_axis=1, tiled=True)  12.9 us
    dot_general x1, matrix products, expert_grads(): jnp.einsum('erf,edf->erd', grad_gate, gate_piece, preferred_element_type=...  12.2 us
  transfers between devices with their start and end apart: 9, of which 3 were waited for; matrix products, arithmetic and copies ran while one was open for 26% of the time, Pallas kernels for 0%

commit v1 on v0

v1 whole, which is shorter than its diff:
```python
import functools
import math

import jax
import jax.numpy as jnp
from jax import lax
from jax.experimental import pallas as pl
from jax.experimental.pallas import tpu as pltpu
from jax.sharding import Mesh
from jax.sharding import PartitionSpec as P

D = 2048
HEADS = 8
HD = 128
EXPERTS = 64
CAP = 10
TOK = 128
RING = 8
RING_AXES = ("zh", "zl")
PLANE_AXES = ("x", "y")
PLANE = 16
HALF_ROWS = EXPERTS * CAP
CHUNKS = 2
F32 = jnp.float32
BF16 = jnp.bfloat16


def ring_shift(value, step):
    return lax.ppermute(value, RING_AXES, [(i, (i + step) % RING) for i in range(RING)])


def swap(value, axis):
    return lax.ppermute(value, axis, [(0, 1), (1, 0)])


def plane_exchange(rows):
    width = rows.shape[1]
    return lax.all_to_all(
        rows.reshape(PLANE, HALF_ROWS // PLANE, width), PLANE_AXES, 0, 0, tiled=True
    ).reshape(HALF_ROWS, width)


def together(*values):
    return lax.optimization_barrier(values)


def route_table(routes, route_gates):
    ids = routes[0]
    experts = jnp.arange(EXPERTS, dtype=jnp.int32)
    named = (ids[:, :, None] == experts).astype(F32)
    table = jnp.sum(named, axis=1)
    position = jnp.arange(TOK, dtype=jnp.int32)
    earlier = (position[None, :] < position[:, None]).astype(BF16)
    before = jnp.dot(earlier, table.astype(BF16), preferred_element_type=F32)
    slot = jnp.sum(named * before[:, None, :], axis=2)
    codes = ids.astype(F32) * 16.0 + slot
    return jnp.concatenate([codes.T, route_gates[0].T], axis=0)


NEAR = (-3, -2, -1, 0, 1, 2, 3)
FAR = (1, 2, 3, 4, -3, -2, -1)
SAVED_ROWS = (256, 256, 128)
MIB = 1024 * 1024


SCALARS = pl.BlockSpec(memory_space=pltpu.SMEM)


def saved_kernel(at_ref, gate_ref, up_ref, own_ref, *outs):
    units = gate_ref.shape[1] // 2
    step = pl.program_id(0)
    first = 0
    for high in range(2):

        @pl.when(at_ref[0] == high)
        def _():
            mine = slice(high * units, (high + 1) * units)
            own_ref[:, :units] = gate_ref[:, mine]
            own_ref[:, units:] = up_ref[:, mine]

    for ref, rows in zip(outs, SAVED_ROWS):
        for high in range(2):

            @pl.when((at_ref[0] == high) & (step >= first) & (step < first + rows // TOK))
            def _():
                other = slice((1 - high) * units, (2 - high) * units)
                ref[:, :units] = gate_ref[:, other]
                ref[:, units:] = up_ref[:, other]

        first += rows // TOK


def split_saved(at, saved_gate, saved_up):
    width = saved_gate.shape[1]
    by_rows = pl.BlockSpec((TOK, width), lambda i: (i, 0))
    parts, shapes, first = [], [], 0
    for rows in SAVED_ROWS:
        count = rows // TOK
        parts.append(
            pl.BlockSpec(
                (TOK, width),
                lambda i, first=first, count=count: (jnp.clip(i - first, 0, count - 1), 0),
            )
        )
        shapes.append(jax.ShapeDtypeStruct((rows, width), BF16))
        first += count
    own, *other = pl.pallas_call(
        saved_kernel,
        grid=(HALF_ROWS // TOK,),
        in_specs=[SCALARS, by_rows, by_rows],
        out_specs=[by_rows, *parts],
        out_shape=[jax.ShapeDtypeStruct(saved_gate.shape, BF16), *shapes],
        compiler_params=pltpu.CompilerParams(vmem_limit_bytes=24 * MIB),
    )(at, saved_gate, saved_up)
    return own, other


def dispatch_kernel(at_ref, *refs):
    tables, blocks = refs[0], refs[1:8]
    rows_ref, select_ref, tokens, row_gate = refs[8:]
    z_low = at_ref[1]

    for low in range(4):

        @pl.when(z_low == low)
        def _():
            for source in range(4):
                tokens[source * TOK : (source + 1) * TOK, :] = blocks[source + 3 - low][...]

        @pl.when((z_low == low) & (pl.program_id(0) == 0))
        def _():
            total = jnp.zeros((HALF_ROWS, 1), F32)
            numbers = lax.broadcasted_iota(jnp.int32, (HALF_ROWS, TOK), 0)
            for source in range(4):
                table = tables[source]
                codes = table[:4].astype(jnp.int32)
                expert = codes >> 4
                row = (expert >> 2) * (4 * CAP) + source * CAP + (codes & 15)
                row = jnp.where((expert & 3) == low, row, -1)
                marks = jnp.zeros((HALF_ROWS, TOK), F32)
                gates = jnp.zeros((HALF_ROWS, TOK), F32)
                for choice in range(4):
                    hit = numbers == row[choice : choice + 1]
                    marks = jnp.where(hit, 1.0, marks)
                    gates = jnp.where(hit, table[4 + choice : 5 + choice], gates)
                select_ref[:, source * TOK : (source + 1) * TOK] = marks.astype(BF16)
                total = total + jnp.sum(gates, axis=1, keepdims=True)
            row_gate[...] = total

    picked = jnp.dot(select_ref[...], tokens[...], preferred_element_type=F32)
    rows_ref[...] = (picked * row_gate[...]).astype(BF16)


def dispatch(at, tables, half, blocks):
    width = 512
    return pl.pallas_call(
        dispatch_kernel,
        grid=(D // width,),
        in_specs=[SCALARS]
        + [pl.BlockSpec((4, 8, TOK), lambda j: (0, 0, 0))]
        + [pl.BlockSpec((TOK, width), lambda j: (0, j))] * 7,
        out_specs=[
            pl.BlockSpec((HALF_ROWS, width), lambda j: (0, j)),
            pl.BlockSpec((HALF_ROWS, 4 * TOK), lambda j: (0, 0)),
        ],
        out_shape=[
            jax.ShapeDtypeStruct((HALF_ROWS, D), BF16),
            jax.ShapeDtypeStruct((HALF_ROWS, 4 * TOK), BF16),
        ],
        scratch_shapes=[pltpu.VMEM((4 * TOK, width), BF16), pltpu.VMEM((HALF_ROWS, 1), F32)],
        compiler_params=pltpu.CompilerParams(vmem_limit_bytes=40 * MIB),
    )(at, lax.dynamic_slice_in_dim(tables, 4 * half, 4, axis=0), *blocks)


def expert_kernel(at_ref, rows_ref, *refs, parts):
    saved, weights, refs = refs[:parts], refs[parts : parts + 6], refs[parts + 6 :]
    *outs, down, gate, up, grad_gate, grad_up, sems = refs
    piece = weights[0].shape[0]
    units = 2 * piece
    step = pl.program_id(0)
    width = outs[0].shape[1]

    @pl.when(step == 0)
    def _():
        copies = []
        for number, ref in enumerate(weights):
            where = at_ref[2] if number % 2 == 0 else 1 - at_ref[2]
            start = pl.multiple_of(where * piece, 16)
            target = (down, gate, up)[number // 2].at[pl.ds(start, piece), :]
            copies.append(pltpu.make_async_copy(ref, target, sems.at[number]))
        for copy in copies:
            copy.start()
        for copy in copies[:2]:
            copy.wait()
        first = 0
        for ref in saved:
            rows = slice(first, first + ref.shape[0])
            first += ref.shape[0]
            hidden_grad = lax.dot_general(
                rows_ref[rows, :],
                down[...],
                (((1,), (1,)), ((), ())),
                preferred_element_type=F32,
            )
            gate_pre = ref[:, :units].astype(F32)
            up_pre = ref[:, units:].astype(F32)
            sigmoid_gate = jax.nn.sigmoid(gate_pre)
            grad_gate[rows, :] = (
                hidden_grad * up_pre * sigmoid_gate * (1.0 + gate_pre * (1.0 - sigmoid_gate))
            ).astype(BF16)
            grad_up[rows, :] = (hidden_grad * gate_pre * sigmoid_gate).astype(BF16)
        for copy in copies[2:]:
            copy.wait()

    columns = pl.ds(pl.multiple_of(step * width, 128), width)
    total = jnp.dot(grad_gate[...], gate[:, columns], preferred_element_type=F32)
    total = total + jnp.dot(grad_up[...], up[:, columns], preferred_element_type=F32)
    total = total.astype(BF16)
    each = pl.num_programs(0) // len(outs)
    for number, out in enumerate(outs):

        @pl.when((step >= number * each) & (step < (number + 1) * each))
        def _():
            out[...] = total


def expert_back(at, rows, saved, weights, chunks):
    steps, each = 4, 4 // chunks
    width = D // steps
    units = saved[0].shape[1] // 2
    constant = lambda value: pl.BlockSpec(value.shape, lambda j: (0, 0))
    return pl.pallas_call(
        functools.partial(expert_kernel, parts=len(saved)),
        grid=(steps,),
        in_specs=[SCALARS, constant(rows)]
        + [constant(part) for part in saved]
        + [pl.BlockSpec(memory_space=pl.ANY)] * len(weights),
        out_specs=[
            pl.BlockSpec(
                (HALF_ROWS, width),
                lambda j, number=number: (0, jnp.clip(j - number * each, 0, each - 1)),
            )
            for number in range(chunks)
        ],
        out_shape=[jax.ShapeDtypeStruct((HALF_ROWS, D // chunks), BF16)] * chunks,
        scratch_shapes=[pltpu.VMEM((units, D), BF16)] * 3
        + [pltpu.VMEM((HALF_ROWS, units), BF16)] * 2
        + [pltpu.SemaphoreType.DMA((len(weights),))],
        compiler_params=pltpu.CompilerParams(vmem_limit_bytes=48 * MIB),
    )(at, rows, *saved, *weights)


def combine(select, returned):
    return lax.dot_general(
        select, returned, (((0,), (0,)), ((), ())), preferred_element_type=F32
    )


class RingSum:
    def __init__(self, own, other, z_high, z_low):
        self.width = own.shape[1]
        self.own, self.other = own, other
        self.z_high, self.z_low = z_high, z_low

    def at(self, step):
        target = (self.z_high * 4 + self.z_low + step + RING) % RING
        start = (target % 4) * TOK
        own, other = (
            lax.dynamic_slice_in_dim(terms, start, TOK, axis=0) for terms in (self.own, self.other)
        )
        return jnp.where(target // 4 == self.z_high, own, other)

    def first(self):
        half = self.width // 2
        far = self.at(4)
        self.up = ring_shift(far[:, :half].astype(BF16), 1)
        self.down = ring_shift(far[:, half:].astype(BF16), -1)

    def next(self, step):
        half = self.width // 2
        ahead, behind = self.at(step), self.at(-step)
        up, down = self.up.astype(F32), self.down.astype(F32)
        if step == 3:
            ahead = jnp.concatenate([ahead[:, :half] + up, ahead[:, half:]], axis=1)
            behind = jnp.concatenate([behind[:, :half], behind[:, half:] + down], axis=1)
        else:
            ahead, behind = ahead + up, behind + down
        self.up = ring_shift(ahead.astype(BF16), 1)
        self.down = ring_shift(behind.astype(BF16), -1)

    def total(self):
        return self.at(0) + self.up.astype(F32) + self.down.astype(F32)


def own_features(value, core):
    a, b, c, d = (value[..., 256 * i : 256 * (i + 1)] for i in range(4))
    first = core == 0
    mine = jnp.concatenate([jnp.where(first, a, b), jnp.where(first, c, d)], axis=-1)
    theirs = jnp.concatenate([jnp.where(first, b, a), jnp.where(first, d, c)], axis=-1)
    return mine, theirs


def all_features(mine, theirs, core):
    first = core == 0
    low, high = slice(0, 256), slice(256, 512)
    return jnp.concatenate(
        [
            jnp.where(first, mine[:, low], theirs[:, low]),
            jnp.where(first, theirs[:, low], mine[:, low]),
            jnp.where(first, mine[:, high], theirs[:, high]),
            jnp.where(first, theirs[:, high], mine[:, high]),
        ],
        axis=1,
    )


def attention_kernel(q_ref, k_ref, v_ref, g_ref, mask_ref, dq_ref, dk_ref, dv_ref, far_ref):
    scale = 1.0 / math.sqrt(HD)
    here = q_ref.shape[0]
    queries, keys, values, grads = q_ref[...], k_ref[...], v_ref[...], g_ref[...]
    last = (((1,), (1,)), ((), ()))
    rows = (((0,), (0,)), ((), ()))
    scores = lax.dot_general(queries, keys, last, preferred_element_type=F32) * scale
    scores = jnp.where(mask_ref[...] > 0.0, scores, -jnp.inf)
    expd = jnp.exp(scores - jnp.max(scores, axis=1, keepdims=True))
    probs = expd / jnp.sum(expd, axis=1, keepdims=True)
    probs_b = probs.astype(BF16)
    attn_out = jnp.dot(probs_b, values, preferred_element_type=F32)
    delta = jnp.sum(grads.astype(F32) * attn_out, axis=1, keepdims=True)
    dprobs = lax.dot_general(grads, values, last, preferred_element_type=F32)
    dscores = (probs * (dprobs - delta)).astype(BF16)
    dq_ref[...] = (jnp.dot(dscores, keys, preferred_element_type=F32) * scale).astype(BF16)
    grad_key = lax.dot_general(dscores, queries, rows, preferred_element_type=F32) * scale
    grad_value = lax.dot_general(probs_b, grads, rows, preferred_element_type=F32)
    dk_ref[...] = grad_key[:here]
    dv_ref[...] = grad_value[:here]
    far_ref[0] = grad_key[here:].astype(BF16)
    far_ref[1] = grad_value[here:].astype(BF16)


def attention_backward(queries, keys, values, grads, mask):
    here, features = queries.shape
    everywhere = keys.shape[0]
    heads = features // HD
    by_head = lambda rows: pl.BlockSpec((rows, HD), lambda h: (0, h))
    return pl.pallas_call(
        attention_kernel,
        grid=(heads,),
        in_specs=[
            by_head(here),
            by_head(everywhere),
            by_head(everywhere),
            by_head(here),
            pl.BlockSpec((here, everywhere), lambda h: (0, 0)),
        ],
        out_specs=[
            by_head(here),
            by_head(here),
            by_head(here),
            pl.BlockSpec((2, here, HD), lambda h: (0, 0, h)),
        ],
        out_shape=[
            jax.ShapeDtypeStruct((here, features), BF16),
            jax.ShapeDtypeStruct((here, features), F32),
            jax.ShapeDtypeStruct((here, features), F32),
            jax.ShapeDtypeStruct((2, here, features), BF16),
        ],
        compiler_params=pltpu.CompilerParams(vmem_limit_bytes=32 * 1024 * 1024),
    )(queries, keys, values, grads, mask)


def on_device(
    query,
    key_states,
    value_states,
    segment_ids,
    out_weight,
    grad_out,
    routes,
    route_gates,
    w_gate,
    w_up,
    w_down,
    saved_gate,
    saved_up,
):
    z_high, core, z_low = lax.axis_index("zh"), lax.axis_index("core"), lax.axis_index("zl")
    plane = lax.axis_index(PLANE_AXES)
    tokens = grad_out[0]

    at = jnp.stack([z_high, z_low, core]).astype(jnp.int32)

    half = TOK // 2
    blocks = {0: tokens}
    blocks[1], blocks[-1] = ring_shift(tokens, -1), ring_shift(tokens, 1)
    table = route_table(routes, route_gates)
    saved_own, saved_leaving = split_saved(at, saved_gate[0], saved_up[0])
    blocks[1], blocks[-1], table = together(blocks[1], blocks[-1], table)

    blocks[2], blocks[-2] = ring_shift(blocks[1], -1), ring_shift(blocks[-1], 1)
    tables = lax.all_to_all(
        jnp.broadcast_to(table[None], (RING, 8, TOK)), RING_AXES, 0, 0, tiled=True
    )
    strip = out_weight.shape[0] // PLANE
    own_strip, _ = together(
        lax.dynamic_slice_in_dim(out_weight, plane * strip, strip, axis=0), table
    )
    fetched = swap(own_strip, "zh")
    blocks[2], blocks[-2], fetched, tables, saved_leaving = together(
        blocks[2], blocks[-2], fetched, tables, saved_leaving
    )

    blocks[3], blocks[-3] = ring_shift(blocks[2], -1), ring_shift(blocks[-2], 1)
    weight_far = lax.all_to_all(
        jnp.broadcast_to(fetched[None], (PLANE, strip, D)), PLANE_AXES, 0, 0, tiled=True
    ).reshape(out_weight.shape)
    blocks[3], blocks[-3], weight_far = together(blocks[3], blocks[-3], weight_far)

    last_up, last_down = ring_shift(blocks[3][:half], -1), ring_shift(blocks[-3][half:], 1)
    leaving_rows, select_own = dispatch(at, tables, z_high, [blocks[i] for i in NEAR])
    rows_own = plane_exchange(leaving_rows)
    last_up, last_down, saved_leaving = together(last_up, last_down, saved_leaving)
    blocks[4] = jnp.concatenate([last_up, last_down], axis=0)
    saved_other = [swap(saved_leaving[0], "zh")]
    leaving_rows, select_other = dispatch(at, tables, 1 - z_high, [blocks[i] for i in FAR])
    weights = []
    for weight in (w_down, w_gate, w_up):
        piece = jnp.swapaxes(weight[0], 0, 1)
        weights += [piece, swap(piece, "core")]

    heads_mine, heads_theirs = [], []
    for value in (query[0], key_states[0], value_states[0]):
        mine, theirs = own_features(value, core)
        heads_mine.append(mine)
        heads_theirs.append(theirs)
    heads_theirs = jnp.concatenate(heads_theirs, axis=1)
    heads_theirs, segment_mine, _ = together(heads_theirs, segment_ids, last_up)
    heads_chip = jnp.concatenate(
        [jnp.concatenate(heads_mine, axis=1), swap(heads_theirs, "core")], axis=0
    )
    segment_chip = jnp.concatenate([segment_mine, swap(segment_mine, "core")], axis=1)
    segment_keys = jnp.concatenate([segment_chip, swap(segment_chip, "zh")], axis=1)[0]
    rows_own, leaving_rows, saved_own, heads_chip, segment_keys, saved_other[0], saved_next = together(
        rows_own, leaving_rows, saved_own, heads_chip, segment_keys, saved_other[0], saved_leaving[1]
    )

    rows_other = plane_exchange(leaving_rows)
    saved_other.append(swap(saved_next, "zh"))
    (leaving_own,) = expert_back(at, rows_own, [saved_own], weights, 1)
    offsets = jnp.arange(TOK, dtype=jnp.int32)
    place = lambda high, which: (high * 2 + which) * TOK + offsets
    chip_place = jnp.concatenate([place(z_high, core), place(z_high, 1 - core)])
    key_place = jnp.concatenate([chip_place, place(1 - z_high, core), place(1 - z_high, 1 - core)])
    segment_here = segment_keys[: 2 * TOK, None]
    causal = key_place[None, :] <= chip_place[:, None]
    image = (segment_here == segment_keys[None, :]) & (segment_here % 2 == 1)
    mask = (causal | image).astype(F32)
    projection = jnp.where(
        z_high == 0,
        jnp.concatenate([out_weight, weight_far], axis=0),
        jnp.concatenate([weight_far, out_weight], axis=0),
    )
    rows_other, leaving_own, mask, projection, saved_other[1], saved_next = together(
        rows_other, leaving_own, mask, projection, saved_other[1], saved_leaving[2]
    )

    back_own = plane_exchange(leaving_own)
    saved_other.append(swap(saved_next, "zh"))
    queries, key_value, saved_other[2] = together(
        heads_chip[:, :512], heads_chip[:, 512:], saved_other[2]
    )
    key_value_far = swap(key_value, "zh")
    leaving = expert_back(at, rows_other, saved_other, weights, CHUNKS)
    width = D // CHUNKS
    columns = [slice(i * width, (i + 1) * width) for i in range(CHUNKS)]
    back_own, leaving = together(back_own, leaving)
    returning = plane_exchange(leaving[0])
    terms_own = combine(select_own, back_own)
    returning, second_leaving, terms_own, key_value_far = together(
        returning, leaving[1], terms_own, key_value_far
    )

    sums = [None, None]
    returning_next = plane_exchange(second_leaving)
    sums[0] = RingSum(terms_own[:, columns[0]], combine(select_other, returning), z_high, z_low)
    sums[0].first()
    sums[0].up, sums[0].down = together(sums[0].up, sums[0].down)
    sums[0].next(3)
    sums[0].up, sums[0].down, returning_next = together(sums[0].up, sums[0].down, returning_next)
    sums[1] = RingSum(
        terms_own[:, columns[1]], combine(select_other, returning_next), z_high, z_low
    )
    sums[0].next(2)
    sums[1].first()

    def meet():
        sums[0].up, sums[0].down, sums[1].up, sums[1].down = together(
            sums[0].up, sums[0].down, sums[1].up, sums[1].down
        )

    meet()
    sums[0].next(1)
    sums[1].next(3)
    meet()
    hidden = []

    def finish(part):
        piece = (tokens[:, columns[part]].astype(F32) + sums[part].total()).astype(BF16)
        hidden.append(piece)
        chip_hidden = jnp.concatenate([piece, swap(piece, "core")], axis=0)
        return lax.dot_general(
            chip_hidden,
            projection[:, columns[part]],
            (((1,), (1,)), ((), ())),
            preferred_element_type=F32,
        )

    sums[1].next(2)
    grad_attn = finish(0)
    sums[1].up, sums[1].down, grad_attn = together(sums[1].up, sums[1].down, grad_attn)
    sums[1].next(1)
    grad_attn = (grad_attn + finish(1)).astype(BF16)
    d_hidden = jnp.concatenate(hidden, axis=1)

    keys = jnp.concatenate([key_value[:, :512], key_value_far[:, :512]], axis=0)
    values = jnp.concatenate([key_value[:, 512:], key_value_far[:, 512:]], axis=0)
    grad_query, grad_key, grad_value, leaving = attention_backward(
        queries, keys, values, grad_attn, mask
    )
    arrived = swap(leaving, "zh").astype(F32)
    outs = []
    for grad in (
        grad_query,
        (grad_key + arrived[0]).astype(BF16),
        (grad_value + arrived[1]).astype(BF16),
    ):
        outs.append(all_features(grad[:TOK], swap(grad[TOK:], "core"), core)[None])
    return (d_hidden[None], *outs)


def solution(mesh):
    fine = Mesh(mesh.devices.reshape(2, 2, 4, 4, 4), ("zh", "core", "x", "y", "zl"))
    exp = ("x", "y", "zl")
    ctx = ("zh", "core")
    in_specs = (
        P(exp, ctx, None),
        P(exp, ctx, None),
        P(exp, ctx, None),
        P(exp, ctx),
        P(ctx, None),
        P(exp, ctx, None),
        P(exp, ctx, None),
        P(exp, ctx, None),
        P(exp, None, ctx),
        P(exp, None, ctx),
        P(exp, None, ctx),
        P(exp, ctx, None),
        P(exp, ctx, None),
    )
    out_specs = (P(exp, ctx, None),) * 4
    return jax.shard_map(
        on_device, mesh=fine, in_specs=in_specs, out_specs=out_specs, check_vma=False
    )
```

time: 604 us -> 367 us (0.61)
  waiting for transfers between devices: 288 us -> 107 us
  starting transfers between devices: 27.8 us -> 149 us
  blocking collectives: 103 us -> 0 us
  local copies, waits for them, and re-layouts: 109 us -> 27.7 us
  Pallas kernels: 0 us -> 40.4 us
  matrix products: 48.3 us -> 10.2 us
  other arithmetic: 11.4 us -> 26.7 us
  between operations: 14.4 us -> 1.86 us
    all_to_all x2 -> x7, waiting for transfers between devices: 235 us -> 6.29 us  [the longest x5 6.28 us: plane_exchange(): lax.all_to_all(rows.reshape(PLANE, HALF_ROWS // PLANE, width), PLANE_AXES...]
    all_gather x1 -> x0, blocking collectives: 103 us -> none  [attention_weights(): lax.all_gather(segment_marks, 'ctx', axis=1, tiled=True)]
    ppermute x0 -> x41, starting transfers between devices: none -> 101 us  [the longest x17 54.8 us: swap(): return lax.ppermute(value, axis, [(0, 1), (1, 0)])]
    ppermute x0 -> x41, waiting for transfers between devices: none -> 101 us  [the longest x24 55.6 us: ring_shift(): lax.ppermute(value, RING_AXES, [(i, (i + step) % RING) for i in range(RIN...]
    scatter x2 -> x0, local copies, waits for them, and re-layouts: 70.9 us -> none  [expert_grads(): outgoing = outgoing.at[local_index, owners, slot_index].set(scaled)]
    reduce_scatter x1 -> x0, waiting for transfers between devices: 50.1 us -> none  [attention_grads(): lax.psum_scatter(jnp.concatenate([key_part.reshape(lax.axis_size('ctx') *...]
    pallas_call x0 -> x6, Pallas kernels: none -> 40.4 us  [the longest x2 25.3 us: expert_back(): pl.pallas_call(functools.partial(expert_kernel, parts=len(saved)), grid=(...]
    dot_general x9 -> x6, matrix products: 44.9 us -> 10.2 us  [the longest x3 9.05 us: combine(): lax.dot_general(select, returned, (((0,), (0,)), ((), ())), preferred_ele...]
  transfers between devices with their start and end apart: 9 -> 48, of which waited for: 3 -> 28; matrix products, arithmetic and copies ran while one was open for 26% -> 10% of each run, Pallas kernels for 0% -> 9%
where the time goes in v1:
time: 367 us; the launch traced here: 363 us
  starting transfers between devices  149 us (41%)
  waiting for transfers between devices  107 us (29%)
  Pallas kernels  40.4 us (11%)
  local copies, waits for them, and re-layouts  27.7 us (8%)
  other arithmetic  26.7 us (7%)
  matrix products  10.2 us (3%)
    ppermute x24, waiting for transfers between devices, ring_shift(): lax.ppermute(value, RING_AXES, [(i, (i + step) % RING) for i in range(RIN...  55.6 us
    ppermute x17, starting transfers between devices, swap(): return lax.ppermute(value, axis, [(0, 1), (1, 0)])  54.8 us
    ppermute x24, starting transfers between devices, ring_shift(): lax.ppermute(value, RING_AXES, [(i, (i + step) % RING) for i in range(RIN...  45.7 us
    ppermute x17, waiting for transfers between devices, swap(): return lax.ppermute(value, axis, [(0, 1), (1, 0)])  44.9 us
    all_to_all x5, starting transfers between devices, plane_exchange(): lax.all_to_all(rows.reshape(PLANE, HALF_ROWS // PLANE, width), PLANE_AXES...  36.5 us
    pallas_call x2, Pallas kernels, expert_back(): pl.pallas_call(functools.partial(expert_kernel, parts=len(saved)), grid=(...  25.3 us
    unnamed x78, local copies, waits for them, and re-layouts  17.1 us
    dot_general x3, matrix products, combine(): lax.dot_general(select, returned, (((0,), (0,)), ((), ())), preferred_ele...  9.05 us
  transfers between devices with their start and end apart: 48, of which 28 were waited for; matrix products, arithmetic and copies ran while one was open for 10% of the time, Pallas kernels for 9%

profile of v1, /device:TPU:1, one launch (start us, length us, event | category | flops | bytes accessed | tf_op | source)
XLA Modules:
  0.0 362.5 jit_solution(996702410366904138)
XLA Ops:
  0.6 6.5 %collective-permute-start = (bf16[128,2048]{1,0:T(8,128)(2,1)}, bf16[128,2048]{1,0:T(8,128)(2,1)S(1)}, u32[]{:S(2)}, u32[]{:S(2)}) collective-permute-start(bf16[128,2048]{1,0:T(8,128)(2,1)} %bitcast.72), channel_id=1, source_target_pairs={{0,131},{1,0},{2,1},{3,2},{128,3},{129,128},{130,129},{131,130},{4... | collective-permute-start | bytes 1572872 | tf_op jit(solution)/shard_map/ppermute | solution.py:29
  10.1 8.0 %collective-permute-done.refs_5_.refs_1_ = bf16[128,2048]{1,0:T(8,128)(2,1)S(1)} collective-permute-done((bf16[128,2048]{1,0:T(8,128)(2,1)}, bf16[128,2048]{1,0:T(8,128)(2,1)S(1)}, u32[]{:S(2)}, u32[]{:S(2)}) %collective-permute-start) | collective-permute-done | bytes 524320 | tf_op jit(solution)/shard_map/ppermute | solution.py:29
  25.7 4.9 %all-to-all-start = ((f32[8,8,128]{2,1,0:T(8,128)}), f32[8,8,128]{2,1,0:T(8,128)S(1)}, u32[]{:S(2)}, u32[]{:S(2)}) async-start(f32[8,8,128]{2,1,0:T(8,128)} %broadcast_in_dim.12), calls=%async_computation | async-start | bytes 65536 | tf_op jit(solution)/shard_map/all_to_all | solution.py:401
  40.0 6.8 %all-to-all-start.1 = ((bf16[16,16,2048]{2,1,0:T(8,128)(2,1)}), bf16[16,16,2048]{2,1,0:T(8,128)(2,1)}, u32[]{:S(2)}, u32[]{:S(2)}) async-start(bf16[16,16,2048]{2,1,0:T(8,128)(2,1)} %broadcast_in_dim.13), calls=%async_computation.1 | async-start | bytes 2097152 | tf_op jit(solution)/shard_map/all_to_all | solution.py:414
  49.6 7.7 %collective-permute-done.5.refs_7_.refs_3_ = bf16[128,2048]{1,0:T(8,128)(2,1)S(1)} collective-permute-done((bf16[128,2048]{1,0:T(8,128)(2,1)S(1)}, bf16[128,2048]{1,0:T(8,128)(2,1)S(1)}, u32[]{:S(2)}, u32[]{:S(2)}) %collective-permute-start.5) | collective-permute-done | bytes 524320 | tf_op jit(solution)/shard_map/ppermute | solution.py:29
  69.3 6.3 %all-to-all-start.2 = ((bf16[16,40,2048]{2,1,0:T(8,128)(2,1)}), bf16[16,40,2048]{2,1,0:T(8,128)(2,1)}, u32[]{:S(2)}, u32[]{:S(2)}) async-start(bf16[16,40,2048]{2,1,0:T(8,128)(2,1)} %bitcast.71), calls=%async_computation.2 | async-start | bytes 5242880 | tf_op jit(solution)/shard_map/all_to_all | solution.py:38
  92.4 21.3 %collective-permute-start.10 = (s32[1,128]{1,0:T(1,128)S(1)}, s32[1,128]{1,0:T(1,128)S(1)}, u32[]{:S(2)}, u32[]{:S(2)}) collective-permute-start(s32[1,128]{1,0:T(1,128)S(1)} %copy-done.38), channel_id=1, source_target_pairs={{0,64},{64,0},{1,65},{65,1},{2,66},{66,2},{3,67},{67,3},{4,68},{68... | collective-permute-start | bytes 1544 | tf_op jit(solution)/shard_map/ppermute | solution.py:33
  114.4 5.7 %collective-permute-start.11 = (s32[1,256]{1,0:T(1,128)S(1)}, s32[1,256]{1,0:T(1,128)S(1)}, u32[]{:S(2)}, u32[]{:S(2)}) collective-permute-start(s32[1,256]{1,0:T(1,128)S(1)} %pad_add_fusion.2), channel_id=1, source_target_pairs={{0,128},{128,0},{1,129},{129,1},{2,130},{130,2},{3,131},{131,3},{4... | collective-permute-start | bytes 3080 | tf_op jit(solution)/shard_map/ppermute | solution.py:33
  127.7 8.5 %all-to-all-start.3 = ((bf16[16,40,2048]{2,1,0:T(8,128)(2,1)}), bf16[16,40,2048]{2,1,0:T(8,128)(2,1)}, u32[]{:S(2)}, u32[]{:S(2)}) async-start(bf16[16,40,2048]{2,1,0:T(8,128)(2,1)} %bitcast.70), calls=%async_computation.3 | async-start | bytes 5242880 | tf_op jit(solution)/shard_map/all_to_all | solution.py:38
  141.6 4.9 %maximum_select_fusion = bf16[512,2048]{1,0:T(8,128)(2,1)} fusion(bf16[256,2048]{1,0:T(8,128)(2,1)} %bitcast.10, bf16[256,2048]{1,0:T(8,128)(2,1)} %param.17, pred[]{:T(512)S(6)} %eq.118), kind=kLoop, calls=%fused_computation | loop fusion | flops 9437184 | bytes 4194305 | tf_op jit(solution)/shard_map/jit(_where)/select_n | solution.py:458
  146.8 12.8 %shard_map.159 = bf16[640,2048]{1,0:T(8,128)(2,1)} custom-call(s32[3]{0:T(128)S(1)} %pad_add_fusion.4.at_ref, bf16[640,2048]{1,0:T(8,128)(2,1)} %bitcast.12.rows_ref, bf16[640,1408]{1,0:T(8,128)(2,1)} %copy-done.9, bf16[352,2048]{1,0:T(8,128)(2,1)S(1)} %bitcast.65, bf16[352,2048]{1,0:T(8,128)(2,1)} %collective-permute-done.13.refs_2_.refs_4_, ...), custom_call_target="tpu_custom_call" | custom-call | tf_op jit(solution)/shard_map/pallas_call | solution.py:232
  159.8 5.9 %collective-permute-done.16.refs_1_ = bf16[256,1408]{1,0:T(8,128)(2,1)S(1)} collective-permute-done((bf16[256,1408]{1,0:T(8,128)(2,1)}, bf16[256,1408]{1,0:T(8,128)(2,1)S(1)}, u32[]{:S(2)}, u32[]{:S(2)}) %collective-permute-start.16) | collective-permute-done | bytes 720928 | tf_op jit(solution)/shard_map/ppermute | solution.py:33
  166.6 8.1 %all-to-all-start.4 = ((bf16[16,40,2048]{2,1,0:T(8,128)(2,1)}), bf16[16,40,2048]{2,1,0:T(8,128)(2,1)}, u32[]{:S(2)}, u32[]{:S(2)}) async-start(bf16[16,40,2048]{2,1,0:T(8,128)(2,1)} %bitcast.80), calls=%async_computation.4 | async-start | bytes 5242880 | tf_op jit(solution)/shard_map/all_to_all | solution.py:38
  179.0 6.8 %collective-permute-done.17.refs_2_ = bf16[128,1408]{1,0:T(8,128)(2,1)S(1)} collective-permute-done((bf16[128,1408]{1,0:T(8,128)(2,1)S(1)}, bf16[128,1408]{1,0:T(8,128)(2,1)S(1)}, u32[]{:S(2)}, u32[]{:S(2)}) %collective-permute-start.17) | collective-permute-done | bytes 360480 | tf_op jit(solution)/shard_map/ppermute | solution.py:33
  188.0 12.6 %shard_map.160 = (bf16[640,1024]{1,0:T(8,128)(2,1)S(1)}, bf16[640,1024]{1,0:T(8,128)(2,1)}) custom-call(s32[3]{0:T(128)S(1)} %pad_add_fusion.4.at_ref, bf16[640,2048]{1,0:T(8,128)(2,1)} %bitcast.18.rows_ref, bf16[256,1408]{1,0:T(8,128)(2,1)S(1)} %copy-done.14, bf16[256,1408]{1,0:T(8,128)(2,1)S(1)} %copy-done.16, ...), custom_call_target="tpu_custom_call" | custom-call | tf_op jit(solution)/shard_map/pallas_call | solution.py:232
  205.1 7.6 %all-to-all-start.5 = ((bf16[16,40,1024]{2,1,0:T(8,128)(2,1)}), bf16[16,40,1024]{2,1,0:T(8,128)(2,1)}, u32[]{:S(2)}, u32[]{:S(2)}) async-start(bf16[16,40,1024]{2,1,0:T(8,128)(2,1)} %bitcast.79), calls=%async_computation.5 | async-start | bytes 2621440 | tf_op jit(solution)/shard_map/all_to_all | solution.py:38
  214.1 5.6 %fusion.29 = f32[512,2048]{1,0:T(8,128)} fusion(bf16[640,512]{1,0:T(8,128)(2,1)S(1)} %copy-done.18, bf16[640,2048]{1,0:T(8,128)(2,1)} %bitcast.29), kind=kOutput, calls=%fused_computation.115 | convolution fusion | flops 1342177280 | bytes 7471104 | tf_op jit(solution)/shard_map/dot_general | solution.py:254
  219.7 7.1 %collective-permute-done.18 = bf16[256,1024]{1,0:T(8,128)(2,1)S(1)} collective-permute-done((bf16[256,1024]{1,0:T(8,128)(2,1)S(1)}, bf16[256,1024]{1,0:T(8,128)(2,1)S(1)}, u32[]{:S(2)}, u32[]{:S(2)}) %collective-permute-start.18) | collective-permute-done | bytes 524320 | tf_op jit(solution)/shard_map/ppermute | solution.py:33
  234.4 6.0 %all-to-all-start.6 = ((bf16[16,40,1024]{2,1,0:T(8,128)(2,1)}), bf16[16,40,1024]{2,1,0:T(8,128)(2,1)S(1)}, u32[]{:S(2)}, u32[]{:S(2)}) async-start(bf16[16,40,1024]{2,1,0:T(8,128)(2,1)} %bitcast.32), calls=%async_computation.6 | async-start | bytes 2621440 | tf_op jit(solution)/shard_map/all_to_all | solution.py:38
  243.1 12.6 %collective-permute-start.20 = (bf16[128,512]{1,0:T(8,128)(2,1)S(1)}, bf16[128,512]{1,0:T(8,128)(2,1)S(1)}, u32[]{:S(2)}, u32[]{:S(2)}) collective-permute-start(bf16[128,512]{1,0:T(8,128)(2,1)S(1)} %get-tuple-element.186), channel_id=1, source_target_pairs={{0,131},{1,0},{2,1},{3,2},{128,3},{129,128},{130,129},{131,130},{4... | collective-permute-start | bytes 393224 | tf_op jit(solution)/shard_map/ppermute | solution.py:29
  291.1 7.2 %collective-permute-start.33 = (bf16[128,1024]{1,0:T(8,128)(2,1)S(1)}, bf16[128,1024]{1,0:T(8,128)(2,1)S(1)}, u32[]{:S(2)}, u32[]{:S(2)}) collective-permute-start(bf16[128,1024]{1,0:T(8,128)(2,1)S(1)} %add_convert_fusion.6), channel_id=1, source_target_pairs={{0,64},{64,0},{1,65},{65,1},{2,66},{66,2},{3,67},{67,3},{4,68},{68... | collective-permute-start | bytes 786440 | tf_op jit(solution)/shard_map/ppermute | solution.py:33
  304.1 6.0 %collective-permute-done.31 = bf16[128,1024]{1,0:T(8,128)(2,1)S(1)} collective-permute-done((bf16[128,1024]{1,0:T(8,128)(2,1)S(1)}, bf16[128,1024]{1,0:T(8,128)(2,1)S(1)}, u32[]{:S(2)}, u32[]{:S(2)}) %collective-permute-start.31) | collective-permute-done | bytes 262176 | tf_op jit(solution)/shard_map/ppermute | solution.py:29
  313.1 5.3 %collective-permute-done.35 = bf16[128,1024]{1,0:T(8,128)(2,1)S(1)} collective-permute-done((bf16[128,1024]{1,0:T(8,128)(2,1)S(1)}, bf16[128,1024]{1,0:T(8,128)(2,1)S(1)}, u32[]{:S(2)}, u32[]{:S(2)}) %collective-permute-start.35) | collective-permute-done | bytes 262176 | tf_op jit(solution)/shard_map/ppermute | solution.py:29
  335.7 22.5 %collective-permute-done.38 = bf16[2,256,512]{2,1,0:T(8,128)(2,1)S(1)} collective-permute-done((bf16[2,256,512]{2,1,0:T(8,128)(2,1)S(1)}, bf16[2,256,512]{2,1,0:T(8,128)(2,1)S(1)}, u32[]{:S(2)}, u32[]{:S(2)}) %collective-permute-start.38) | collective-permute-done | bytes 524320 | tf_op jit(solution)/shard_map/ppermute | solution.py:33
  (237 shorter events, 154.3 us)
Async XLA Ops:
  0.6 17.4 %collective-permute-start = (bf16[128,2048]{1,0:T(8,128)(2,1)}, bf16[128,2048]{1,0:T(8,128)(2,1)S(1)}, u32[]{:S(2)}, u32[]{:S(2)}) collective-permute-start(bf16[128,2048]{1,0:T(8,128)(2,1)} %bitcast.72), channel_id=1, source_target_pairs={{0,131},{1,0},{2,1},{3,2},{128,3},{129,128},{130,129},{131,130},{4... | collective-permute-start | bytes 1572872 | tf_op jit(solution)/shard_map/ppermute | solution.py:29
  7.1 13.9 %collective-permute-start.1 = (bf16[128,2048]{1,0:T(8,128)(2,1)}, bf16[128,2048]{1,0:T(8,128)(2,1)S(1)}, u32[]{:S(2)}, u32[]{:S(2)}) collective-permute-start(bf16[128,2048]{1,0:T(8,128)(2,1)} %bitcast.73), channel_id=1, source_target_pairs={{0,1},{1,2},{2,3},{3,128},{128,129},{129,130},{130,131},{131,0},{4... | collective-permute-start | bytes 1572872 | tf_op jit(solution)/shard_map/ppermute | solution.py:29
  21.0 17.8 %collective-permute-start.2 = (bf16[128,2048]{1,0:T(8,128)(2,1)S(1)}, bf16[128,2048]{1,0:T(8,128)(2,1)S(1)}, u32[]{:S(2)}, u32[]{:S(2)}) collective-permute-start(bf16[128,2048]{1,0:T(8,128)(2,1)S(1)} %collective-permute-done.refs_5_.refs_1_), channel_id=1, source_target_pairs={{0,131},{1,0},{2,1},{3,2},{128,3},{129,128},{130,129},{131,130},{4... | collective-permute-start | bytes 1572872 | tf_op jit(solution)/shard_map/ppermute | solution.py:29
  21.3 17.5 %collective-permute-start.3 = (bf16[128,2048]{1,0:T(8,128)(2,1)S(1)}, bf16[128,2048]{1,0:T(8,128)(2,1)S(1)}, u32[]{:S(2)}, u32[]{:S(2)}) collective-permute-start(bf16[128,2048]{1,0:T(8,128)(2,1)S(1)} %collective-permute-done.1.refs_3_.refs_7_), channel_id=1, source_target_pairs={{0,1},{1,2},{2,3},{3,128},{128,129},{129,130},{130,131},{131,0},{4... | collective-permute-start | bytes 1572872 | tf_op jit(solution)/shard_map/ppermute | solution.py:29
  23.3 15.5 %collective-permute-start.4 = (bf16[16,2048]{1,0:T(8,128)(2,1)S(1)}, bf16[16,2048]{1,0:T(8,128)(2,1)S(1)}, u32[]{:S(2)}, u32[]{:S(2)}) collective-permute-start(bf16[16,2048]{1,0:T(8,128)(2,1)S(1)} %constant_dynamic-slice_fusion.2), channel_id=1, source_target_pairs={{0,128},{128,0},{1,129},{129,1},{2,130},{130,2},{3,131},{131,3},{4... | collective-permute-start | bytes 196616 | tf_op jit(solution)/shard_map/ppermute | solution.py:33
  25.7 13.1 %all-to-all-start = ((f32[8,8,128]{2,1,0:T(8,128)}), f32[8,8,128]{2,1,0:T(8,128)S(1)}, u32[]{:S(2)}, u32[]{:S(2)}) async-start(f32[8,8,128]{2,1,0:T(8,128)} %broadcast_in_dim.12), calls=%async_computation | async-start | bytes 65536 | tf_op jit(solution)/shard_map/all_to_all | solution.py:401
  40.0 20.7 %all-to-all-start.1 = ((bf16[16,16,2048]{2,1,0:T(8,128)(2,1)}), bf16[16,16,2048]{2,1,0:T(8,128)(2,1)}, u32[]{:S(2)}, u32[]{:S(2)}) async-start(bf16[16,16,2048]{2,1,0:T(8,128)(2,1)} %broadcast_in_dim.13), calls=%async_computation.1 | async-start | bytes 2097152 | tf_op jit(solution)/shard_map/all_to_all | solution.py:414
  49.6 11.1 %collective-permute-start.6 = (bf16[128,2048]{1,0:T(8,128)(2,1)}, bf16[128,2048]{1,0:T(8,128)(2,1)S(1)}, u32[]{:S(2)}, u32[]{:S(2)}) collective-permute-start(bf16[128,2048]{1,0:T(8,128)(2,1)} %copy-done.4), channel_id=1, source_target_pairs={{0,1},{1,2},{2,3},{3,128},{128,129},{129,130},{130,131},{131,0},{4... | collective-permute-start | bytes 1572872 | tf_op jit(solution)/shard_map/ppermute | solution.py:29
  69.3 58.4 %all-to-all-start.2 = ((bf16[16,40,2048]{2,1,0:T(8,128)(2,1)}), bf16[16,40,2048]{2,1,0:T(8,128)(2,1)}, u32[]{:S(2)}, u32[]{:S(2)}) async-start(bf16[16,40,2048]{2,1,0:T(8,128)(2,1)} %bitcast.71), calls=%async_computation.2 | async-start | bytes 5242880 | tf_op jit(solution)/shard_map/all_to_all | solution.py:38
  89.3 37.5 %collective-permute-start.12 = (bf16[256,1408]{1,0:T(8,128)(2,1)S(1)}, bf16[256,1408]{1,0:T(8,128)(2,1)S(1)}, u32[]{:S(2)}, u32[]{:S(2)}) collective-permute-start(bf16[256,1408]{1,0:T(8,128)(2,1)S(1)} %copy-done.21), channel_id=1, source_target_pairs={{0,128},{128,0},{1,129},{129,1},{2,130},{130,2},{3,131},{131,3},{4... | collective-permute-start | bytes 2162696 | tf_op jit(solution)/shard_map/ppermute | solution.py:33
  92.4 22.1 %collective-permute-start.10 = (s32[1,128]{1,0:T(1,128)S(1)}, s32[1,128]{1,0:T(1,128)S(1)}, u32[]{:S(2)}, u32[]{:S(2)}) collective-permute-start(s32[1,128]{1,0:T(1,128)S(1)} %copy-done.38), channel_id=1, source_target_pairs={{0,64},{64,0},{1,65},{65,1},{2,66},{66,2},{3,67},{67,3},{4,68},{68... | collective-permute-start | bytes 1544 | tf_op jit(solution)/shard_map/ppermute | solution.py:33
  113.6 12.3 %collective-permute-start.9 = (bf16[128,1536]{1,0:T(8,128)(2,1)S(1)}, bf16[128,1536]{1,0:T(8,128)(2,1)S(1)}, u32[]{:S(2)}, u32[]{:S(2)}) collective-permute-start(bf16[128,1536]{1,0:T(8,128)(2,1)S(1)} %select_dynamic-update-slice_fusion), channel_id=1, source_target_pairs={{0,64},{64,0},{1,65},{65,1},{2,66},{66,2},{3,67},{67,3},{4,68},{68... | collective-permute-start | bytes 1179656 | tf_op jit(solution)/shard_map/ppermute | solution.py:33
  114.4 11.4 %collective-permute-start.11 = (s32[1,256]{1,0:T(1,128)S(1)}, s32[1,256]{1,0:T(1,128)S(1)}, u32[]{:S(2)}, u32[]{:S(2)}) collective-permute-start(s32[1,256]{1,0:T(1,128)S(1)} %pad_add_fusion.2), channel_id=1, source_target_pairs={{0,128},{128,0},{1,129},{129,1},{2,130},{130,2},{3,131},{131,3},{4... | collective-permute-start | bytes 3080 | tf_op jit(solution)/shard_map/ppermute | solution.py:33
  127.7 38.9 %all-to-all-start.3 = ((bf16[16,40,2048]{2,1,0:T(8,128)(2,1)}), bf16[16,40,2048]{2,1,0:T(8,128)(2,1)}, u32[]{:S(2)}, u32[]{:S(2)}) async-start(bf16[16,40,2048]{2,1,0:T(8,128)(2,1)} %bitcast.70), calls=%async_computation.3 | async-start | bytes 5242880 | tf_op jit(solution)/shard_map/all_to_all | solution.py:38
  140.0 25.7 %collective-permute-start.16 = (bf16[256,1408]{1,0:T(8,128)(2,1)}, bf16[256,1408]{1,0:T(8,128)(2,1)S(1)}, u32[]{:S(2)}, u32[]{:S(2)}) collective-permute-start(bf16[256,1408]{1,0:T(8,128)(2,1)} %copy-done.19), channel_id=1, source_target_pairs={{0,128},{128,0},{1,129},{129,1},{2,130},{130,2},{3,131},{131,3},{4... | collective-permute-start | bytes 2162696 | tf_op jit(solution)/shard_map/ppermute | solution.py:33
  166.6 38.5 %all-to-all-start.4 = ((bf16[16,40,2048]{2,1,0:T(8,128)(2,1)}), bf16[16,40,2048]{2,1,0:T(8,128)(2,1)}, u32[]{:S(2)}, u32[]{:S(2)}) async-start(bf16[16,40,2048]{2,1,0:T(8,128)(2,1)} %bitcast.80), calls=%async_computation.4 | async-start | bytes 5242880 | tf_op jit(solution)/shard_map/all_to_all | solution.py:38
  205.1 24.4 %all-to-all-start.5 = ((bf16[16,40,1024]{2,1,0:T(8,128)(2,1)}), bf16[16,40,1024]{2,1,0:T(8,128)(2,1)}, u32[]{:S(2)}, u32[]{:S(2)}) async-start(bf16[16,40,1024]{2,1,0:T(8,128)(2,1)} %bitcast.79), calls=%async_computation.5 | async-start | bytes 2621440 | tf_op jit(solution)/shard_map/all_to_all | solution.py:38
  212.7 14.1 %collective-permute-start.18 = (bf16[256,1024]{1,0:T(8,128)(2,1)S(1)}, bf16[256,1024]{1,0:T(8,128)(2,1)S(1)}, u32[]{:S(2)}, u32[]{:S(2)}) collective-permute-start(bf16[256,1024]{1,0:T(8,128)(2,1)S(1)} %copy-done.33), channel_id=1, source_target_pairs={{0,128},{128,0},{1,129},{129,1},{2,130},{130,2},{3,131},{131,3},{4... | collective-permute-start | bytes 1572872 | tf_op jit(solution)/shard_map/ppermute | solution.py:33
  234.4 31.8 %all-to-all-start.6 = ((bf16[16,40,1024]{2,1,0:T(8,128)(2,1)}), bf16[16,40,1024]{2,1,0:T(8,128)(2,1)S(1)}, u32[]{:S(2)}, u32[]{:S(2)}) async-start(bf16[16,40,1024]{2,1,0:T(8,128)(2,1)} %bitcast.32), calls=%async_computation.6 | async-start | bytes 2621440 | tf_op jit(solution)/shard_map/all_to_all | solution.py:38
  243.0 15.2 %collective-permute-start.19 = (bf16[128,512]{1,0:T(8,128)(2,1)S(1)}, bf16[128,512]{1,0:T(8,128)(2,1)S(1)}, u32[]{:S(2)}, u32[]{:S(2)}) collective-permute-start(bf16[128,512]{1,0:T(8,128)(2,1)S(1)} %get-tuple-element.187), channel_id=1, source_target_pairs={{0,1},{1,2},{2,3},{3,128},{128,129},{129,130},{130,131},{131,0},{4... | collective-permute-start | bytes 393224 | tf_op jit(solution)/shard_map/ppermute | solution.py:29
  243.1 15.1 %collective-permute-start.20 = (bf16[128,512]{1,0:T(8,128)(2,1)S(1)}, bf16[128,512]{1,0:T(8,128)(2,1)S(1)}, u32[]{:S(2)}, u32[]{:S(2)}) collective-permute-start(bf16[128,512]{1,0:T(8,128)(2,1)S(1)} %get-tuple-element.186), channel_id=1, source_target_pairs={{0,131},{1,0},{2,1},{3,2},{128,3},{129,128},{130,129},{131,130},{4... | collective-permute-start | bytes 393224 | tf_op jit(solution)/shard_map/ppermute | solution.py:29
  291.1 12.4 %collective-permute-start.33 = (bf16[128,1024]{1,0:T(8,128)(2,1)S(1)}, bf16[128,1024]{1,0:T(8,128)(2,1)S(1)}, u32[]{:S(2)}, u32[]{:S(2)}) collective-permute-start(bf16[128,1024]{1,0:T(8,128)(2,1)S(1)} %add_convert_fusion.6), channel_id=1, source_target_pairs={{0,64},{64,0},{1,65},{65,1},{2,66},{66,2},{3,67},{67,3},{4,68},{68... | collective-permute-start | bytes 786440 | tf_op jit(solution)/shard_map/ppermute | solution.py:33
  329.8 28.4 %collective-permute-start.38 = (bf16[2,256,512]{2,1,0:T(8,128)(2,1)S(1)}, bf16[2,256,512]{2,1,0:T(8,128)(2,1)S(1)}, u32[]{:S(2)}, u32[]{:S(2)}) collective-permute-start(bf16[2,256,512]{2,1,0:T(8,128)(2,1)S(1)} %get-tuple-element.150), channel_id=1, source_target_pairs={{0,128},{128,0},{1,129},{129,1},{2,130},{130,2},{3,131},{131,3},{4... | collective-permute-start | bytes 1572872 | tf_op jit(solution)/shard_map/ppermute | solution.py:33
  334.9 24.2 %collective-permute-start.37 = (bf16[128,512]{1,0:T(8,128)(2,1)S(1)}, bf16[128,512]{1,0:T(8,128)(2,1)S(1)}, u32[]{:S(2)}, u32[]{:S(2)}) collective-permute-start(bf16[128,512]{1,0:T(8,128)(2,1)S(1)} %slice.237), channel_id=1, source_target_pairs={{0,64},{64,0},{1,65},{65,1},{2,66},{66,2},{3,67},{67,3},{4,68},{68... | collective-permute-start | bytes 393224 | tf_op jit(solution)/shard_map/ppermute | solution.py:33
  (63 other events, 442.1 us)
